TPU v7x, 32 devices: a whole 2x2x4 slice. The times are simulated.
32 devices in a mesh: dp: 8 (over y, x, core), sp: 4 (over z).
Axes of the slice: x: 2, y: 2, z: 4, core: 2. Of those that a mesh axis runs over, the one named last changes fastest.
Arguments:
- inputs: bfloat16 [8, 2048, 512], P('dp', 'sp'), may hold values from -6 to 6
- encoder: bfloat16 [8, 2048, 512], P('dp', 'sp'), may hold values from -6 to 6
- cotangent: bfloat16 [8, 2048, 512], P('dp', 'sp'), may hold values from -6 to 6
- w_self: bfloat16 [512, 1536], P('dp'), may hold values from -0.375 to 0.375
- w_self_out: bfloat16 [512, 512], P('dp'), may hold values from -0.75 to 0.75
- w_cross_q: bfloat16 [512, 512], P('dp'), may hold values from -0.375 to 0.375
- w_cross_kv: bfloat16 [512, 1024], P('dp'), may hold values from -0.375 to 0.375
- w_cross_out: bfloat16 [512, 512], P('dp'), may hold values from -0.75 to 0.75
- w_up: bfloat16 [512, 2048], P('dp'), may hold values from -0.25 to 0.25
- w_down: bfloat16 [2048, 512], P('dp'), may hold values from -0.1875 to 0.1875
- biases: bfloat16 [10, 512], P(None, 'dp'), may hold values from -1.5 to 1.5
- norm_gains: bfloat16 [3, 512], P(None, 'dp'), may hold values from 0.25 to 1.75
- up_bias: bfloat16 [2048], P('dp'), may hold values from -1.5 to 1.5
- source_lengths: int32 [8], P('dp'), may hold values from 512 to 2048, as said below
Outputs:
- output: bfloat16 [8, 2048, 512], P('dp', 'sp')
- grad_inputs: float32 [8, 2048, 512], P('dp', 'sp')
- grad_encoder: float32 [8, 2048, 512], P('dp', 'sp')
- grad_w_self: float32 [512, 1536], P('dp', 'sp')
- grad_w_self_out: float32 [512, 512], P('dp', 'sp')
- grad_w_cross_q: float32 [512, 512], P('dp', 'sp')
- grad_w_cross_kv: float32 [512, 1024], P('dp', 'sp')
- grad_w_cross_out: float32 [512, 512], P('dp', 'sp')
- grad_w_up: float32 [512, 2048], P('dp', 'sp')
- grad_w_down: float32 [2048, 512], P('dp', 'sp')
- grad_biases: float32 [10, 512], P(None, ('dp', 'sp'))
- grad_gains: float32 [3, 512], P(None, ('dp', 'sp'))
- grad_up_bias: float32 [2048], P(('dp', 'sp'))
Inputs may be any that keep to these rules, and one draw needn't show every extreme that they name: Sequence s attends to encoder states 0 to source_lengths[s] - 1; in every draw some sequence has all 2048.
All inputs are finite; a program needn't handle non-finite values.
Results may differ from a plain program's by a relative error of at most 0.025.
The roundings to bfloat16 on the way count: a program that leaves them out, or rounds other values in their place, can miss the bound.
Values may be sent and summed in bfloat16 or wider, within the bound.
No kernel may reach another device: no remote copies, remote signals or barrier semaphores. Data moves between devices by JAX's collectives and lax.ppermute only.
A program may use at most 128 MiB of HBM per device.

v0:
```python
import jax
import jax.numpy as jnp
from jax import lax
from jax.sharding import PartitionSpec as P

H = 8
DH = 64


eps_norm = 1e-05
masked_out = -1e30


def matmul(left, right):
    return jnp.dot(left, right, preferred_element_type=jnp.float32)


def tmatmul(left, right):
    return lax.dot_general(
        left, right, (((0,), (0,)), ((), ())), preferred_element_type=jnp.float32
    )


def right_trans(left, right):
    return lax.dot_general(
        left, right, (((1,), (1,)), ((), ())), preferred_element_type=jnp.float32
    )


def norm_forward(resid, gain, shift):
    centred = resid - jnp.mean(resid, axis=-1, keepdims=True)
    inv_std = lax.rsqrt(jnp.mean(centred * centred, axis=-1, keepdims=True) + eps_norm)
    normed = centred * inv_std
    return (normed * gain + shift, normed, inv_std)


def norm_backward(upstream, normed, inv_std, gain):
    scaled = upstream * gain
    centre_term = jnp.mean(scaled, axis=-1, keepdims=True)
    slope_term = jnp.mean(scaled * normed, axis=-1, keepdims=True)
    result = inv_std * (scaled - centre_term - normed * slope_term)
    return (result, jnp.sum(upstream * normed, axis=0), jnp.sum(upstream, axis=0))


def attend_forward(queries, key_rows, value_rows, allowed):
    length = queries.shape[0]
    step_rows = min(512, length)

    def one_block(first_row):
        query_block = lax.dynamic_slice_in_dim(queries, first_row, step_rows, 0)
        scores = jnp.einsum(
            "qhe,khe->hqk", query_block, key_rows, preferred_element_type=jnp.float32
        )
        scores = jnp.where(allowed(first_row, step_rows)[None], scores, masked_out)
        row_max = jnp.max(scores, axis=-1, keepdims=True)
        raised = jnp.exp(scores - row_max)
        row_sum = jnp.sum(raised, axis=-1, keepdims=True)
        probs_low = (raised / row_sum).astype(jnp.bfloat16)
        result = jnp.einsum(
            "hqk,khe->qhe", probs_low, value_rows, preferred_element_type=jnp.float32
        )
        return (result, (row_max + jnp.log(row_sum))[..., 0])

    starts = jnp.arange(length // step_rows, dtype=jnp.int32) * step_rows
    results, log_sums = lax.map(one_block, starts)
    return (results.reshape(queries.shape), log_sums)


def attend_backward(queries, key_rows, value_rows, grad_out, log_sums, allowed):
    length = queries.shape[0]
    step_rows = min(512, length)

    def one_block(carry, entry):
        first_row, block_sums = entry
        query_block = lax.dynamic_slice_in_dim(queries, first_row, step_rows, 0)
        grad_block = lax.dynamic_slice_in_dim(grad_out, first_row, step_rows, 0)
        scores = jnp.einsum(
            "qhe,khe->hqk", query_block, key_rows, preferred_element_type=jnp.float32
        )
        probs = jnp.where(
            allowed(first_row, step_rows)[None], jnp.exp(scores - block_sums[..., None]), 0.0
        )
        grad_probs = jnp.einsum(
            "qhe,khe->hqk", grad_block, value_rows, preferred_element_type=jnp.float32
        )
        row_delta = jnp.sum(probs * grad_probs, axis=-1, keepdims=True)
        grad_scores = (probs * (grad_probs - row_delta)).astype(jnp.bfloat16)
        grad_query = jnp.einsum(
            "hqk,khe->qhe", grad_scores, key_rows, preferred_element_type=jnp.float32
        )
        grad_keys = carry[0] + jnp.einsum(
            "hqk,qhe->khe", grad_scores, query_block, preferred_element_type=jnp.float32
        )
        grad_values = carry[1] + jnp.einsum(
            "hqk,qhe->khe",
            probs.astype(jnp.bfloat16),
            grad_block,
            preferred_element_type=jnp.float32,
        )
        return ((grad_keys, grad_values), grad_query)

    starts = jnp.arange(length // step_rows, dtype=jnp.int32) * step_rows
    empty = jnp.zeros(key_rows.shape, jnp.float32)
    (grad_keys, grad_values), grad_queries = lax.scan(one_block, (empty, empty), (starts, log_sums))
    return (grad_queries.reshape(queries.shape), grad_keys, grad_values)


def on_device(
    inputs,
    encoder,
    cotangent,
    w_self,
    w_self_out,
    w_cross_q,
    w_cross_kv,
    w_cross_out,
    w_up,
    w_down,
    biases,
    norm_gains,
    up_bias,
    source_lengths,
):
    seq_local, tok_local, model_width = inputs.shape
    src_local = encoder.shape[1]
    sp_count = lax.axis_size("sp")
    dp_count = lax.axis_size("dp")
    head_width = model_width // sp_count
    heads_here = H // sp_count
    query_scale = DH ** (-0.5)
    tokens = seq_local * tok_local
    sources = seq_local * src_local
    (
        full_self,
        full_self_out,
        full_cross_q,
        full_cross_kv,
        full_cross_out,
        full_up,
        full_down,
        full_bias,
        full_gains,
        full_up_bias,
    ) = (
        lax.all_gather(w_self, "dp", axis=0, tiled=True),
        lax.all_gather(w_self_out, "dp", axis=0, tiled=True),
        lax.all_gather(w_cross_q, "dp", axis=0, tiled=True),
        lax.all_gather(w_cross_kv, "dp", axis=0, tiled=True),
        lax.all_gather(w_cross_out, "dp", axis=0, tiled=True),
        lax.all_gather(w_up, "dp", axis=0, tiled=True),
        lax.all_gather(w_down, "dp", axis=0, tiled=True),
        lax.all_gather(biases, "dp", axis=1, tiled=True),
        lax.all_gather(norm_gains, "dp", axis=1, tiled=True),
        lax.all_gather(up_bias, "dp", axis=0, tiled=True),
    )
    bias_rows = full_bias.astype(jnp.float32)
    gain_rows = full_gains.astype(jnp.float32)
    up_shift = full_up_bias.astype(jnp.float32)
    zero_row = jnp.zeros((model_width,), jnp.float32)
    flat_in = inputs.reshape(tokens, model_width)
    flat_enc = encoder.reshape(sources, model_width)
    qkv_shift = jnp.stack([bias_rows[0], zero_row, bias_rows[1]])
    qkv_scale = jnp.array([query_scale, 1.0, 1.0], jnp.float32)[:, None]
    self_proj = (
        (matmul(flat_in, full_self).reshape(tokens, 3, model_width) + qkv_shift) * qkv_scale
    ).astype(jnp.bfloat16)
    encoder_proj = (
        matmul(flat_enc, full_cross_kv).reshape(sources, 2, model_width)
        + jnp.stack([zero_row, bias_rows[4]])
    ).astype(jnp.bfloat16)
    self_heads, enc_heads = (
        lax.all_to_all(
            self_proj.reshape(seq_local, tok_local, 3, model_width),
            "sp",
            split_axis=3,
            concat_axis=1,
            tiled=True,
        ),
        lax.all_to_all(
            encoder_proj.reshape(seq_local, src_local, 2, model_width),
            "sp",
            split_axis=3,
            concat_axis=1,
            tiled=True,
        ),
    )
    length = self_heads.shape[1]
    src_full = enc_heads.shape[1]

    def split_heads(block):
        return block.reshape(block.shape[0], heads_here, DH)

    def causal(first_row, count):
        query_pos = first_row + jnp.arange(count, dtype=jnp.int32)[:, None]
        return jnp.arange(length, dtype=jnp.int32)[None, :] <= query_pos

    def self_forward(sequence):
        return attend_forward(
            split_heads(sequence[:, 0]),
            split_heads(sequence[:, 1]),
            split_heads(sequence[:, 2]),
            causal,
        )

    self_att, self_sums = lax.map(self_forward, self_heads)
    self_back = lax.all_to_all(
        self_att.reshape(seq_local, length, head_width).astype(jnp.bfloat16),
        "sp",
        split_axis=1,
        concat_axis=2,
        tiled=True,
    )
    self_tokens = self_back.reshape(tokens, model_width)
    resid_one = flat_in.astype(jnp.float32) + matmul(self_tokens, full_self_out) + bias_rows[2]
    hidden_one, normed_one, inv_one = norm_forward(resid_one, gain_rows[0], bias_rows[7])
    hidden_one_low = hidden_one.astype(jnp.bfloat16)
    cross_proj = ((matmul(hidden_one_low, full_cross_q) + bias_rows[3]) * query_scale).astype(
        jnp.bfloat16
    )
    cross_heads = lax.all_to_all(
        cross_proj.reshape(seq_local, tok_local, model_width),
        "sp",
        split_axis=2,
        concat_axis=1,
        tiled=True,
    )

    def seen_keys(source_limit):

        def visible(first_row, count):
            return jnp.broadcast_to(
                jnp.arange(src_full, dtype=jnp.int32)[None, :] < source_limit, (count, src_full)
            )

        return visible

    def cross_forward(sequence):
        queries, enc_pair, source_limit = sequence
        return attend_forward(
            split_heads(queries),
            split_heads(enc_pair[:, 0]),
            split_heads(enc_pair[:, 1]),
            seen_keys(source_limit),
        )

    cross_att, cross_sums = lax.map(cross_forward, (cross_heads, enc_heads, source_lengths))
    cross_back = lax.all_to_all(
        cross_att.reshape(seq_local, length, head_width).astype(jnp.bfloat16),
        "sp",
        split_axis=1,
        concat_axis=2,
        tiled=True,
    )
    cross_tokens = cross_back.reshape(tokens, model_width)
    resid_two = hidden_one + matmul(cross_tokens, full_cross_out) + bias_rows[5]
    hidden_two, normed_two, inv_two = norm_forward(resid_two, gain_rows[1], bias_rows[8])
    hidden_two_low = hidden_two.astype(jnp.bfloat16)
    up_value = matmul(hidden_two_low, full_up) + up_shift
    activation = jax.nn.silu(up_value).astype(jnp.bfloat16)
    resid_three = hidden_two + matmul(activation, full_down) + bias_rows[6]
    result, normed_three, inv_three = norm_forward(resid_three, gain_rows[2], bias_rows[9])
    output = result.astype(jnp.bfloat16).reshape(inputs.shape)
    (
        back_self,
        back_self_out,
        back_cross_q,
        back_cross_kv,
        back_cross_out,
        back_up,
        back_down,
        back_gains,
    ) = (
        lax.all_gather(w_self, "dp", axis=0, tiled=True),
        lax.all_gather(w_self_out, "dp", axis=0, tiled=True),
        lax.all_gather(w_cross_q, "dp", axis=0, tiled=True),
        lax.all_gather(w_cross_kv, "dp", axis=0, tiled=True),
        lax.all_gather(w_cross_out, "dp", axis=0, tiled=True),
        lax.all_gather(w_up, "dp", axis=0, tiled=True),
        lax.all_gather(w_down, "dp", axis=0, tiled=True),
        lax.all_gather(norm_gains, "dp", axis=1, tiled=True),
    )
    back_gain_rows = back_gains.astype(jnp.float32)
    upstream = cotangent.reshape(tokens, model_width).astype(jnp.float32)
    grad_three, gain_three, shift_three = norm_backward(
        upstream, normed_three, inv_three, back_gain_rows[2]
    )
    down_low = grad_three.astype(jnp.bfloat16)
    grad_down = tmatmul(activation, down_low)
    grad_activation = right_trans(down_low, back_down)
    sigmoid_up = jax.nn.sigmoid(up_value)
    up_low = (grad_activation * sigmoid_up * (1.0 + up_value * (1.0 - sigmoid_up))).astype(
        jnp.bfloat16
    )
    grad_up = tmatmul(hidden_two_low, up_low)
    grad_up_bias = jnp.sum(up_low.astype(jnp.float32), axis=0)
    grad_hidden_two = grad_three + right_trans(up_low, back_up)
    grad_two, gain_two, shift_two = norm_backward(
        grad_hidden_two, normed_two, inv_two, back_gain_rows[1]
    )
    cross_low = grad_two.astype(jnp.bfloat16)
    grad_cross_out = tmatmul(cross_tokens, cross_low)
    cross_grad = right_trans(cross_low, back_cross_out).astype(jnp.bfloat16)
    cross_grad_heads = lax.all_to_all(
        cross_grad.reshape(seq_local, tok_local, model_width),
        "sp",
        split_axis=2,
        concat_axis=1,
        tiled=True,
    )

    def cross_backward(sequence):
        queries, enc_pair, source_limit, grad_out, log_sums = sequence
        grad_query, grad_keys, grad_values = attend_backward(
            split_heads(queries),
            split_heads(enc_pair[:, 0]),
            split_heads(enc_pair[:, 1]),
            split_heads(grad_out),
            log_sums,
            seen_keys(source_limit),
        )
        key_value = jnp.stack(
            [grad_keys.reshape(src_full, head_width), grad_values.reshape(src_full, head_width)],
            axis=1,
        )
        return (
            grad_query.reshape(length, 1, head_width).astype(jnp.bfloat16),
            key_value.astype(jnp.bfloat16),
        )

    cross_dq, enc_dkv = lax.map(
        cross_backward, (cross_heads, enc_heads, source_lengths, cross_grad_heads, cross_sums)
    )
    query_back, enc_back = (
        lax.all_to_all(cross_dq, "sp", split_axis=1, concat_axis=3, tiled=True),
        lax.all_to_all(enc_dkv, "sp", split_axis=1, concat_axis=3, tiled=True),
    )
    query_grad = query_back.reshape(tokens, model_width) * query_scale
    grad_cross_q = tmatmul(hidden_one_low, query_grad)
    grad_hidden_one = grad_two + right_trans(query_grad, back_cross_q)
    enc_grad = enc_back.reshape(sources, 2 * model_width)
    grad_cross_kv = tmatmul(flat_enc, enc_grad)
    grad_encoder = right_trans(enc_grad, back_cross_kv).reshape(encoder.shape)
    enc_value_sum = jnp.sum(
        enc_back.reshape(sources, 2, model_width)[:, 1].astype(jnp.float32), axis=0
    )
    grad_one, gain_one, shift_one = norm_backward(
        grad_hidden_one, normed_one, inv_one, back_gain_rows[0]
    )
    self_low = grad_one.astype(jnp.bfloat16)
    grad_self_out = tmatmul(self_tokens, self_low)
    self_grad = right_trans(self_low, back_self_out).astype(jnp.bfloat16)
    self_grad_heads = lax.all_to_all(
        self_grad.reshape(seq_local, tok_local, model_width),
        "sp",
        split_axis=2,
        concat_axis=1,
        tiled=True,
    )

    def self_backward(sequence):
        triple, grad_out, log_sums = sequence
        grad_query, grad_keys, grad_values = attend_backward(
            split_heads(triple[:, 0]),
            split_heads(triple[:, 1]),
            split_heads(triple[:, 2]),
            split_heads(grad_out),
            log_sums,
            causal,
        )
        merged = jnp.stack(
            [
                grad_query.reshape(length, head_width),
                grad_keys.reshape(length, head_width),
                grad_values.reshape(length, head_width),
            ],
            axis=1,
        )
        return merged.astype(jnp.bfloat16)

    self_dqkv = lax.map(self_backward, (self_heads, self_grad_heads, self_sums))
    qkv_back = lax.all_to_all(self_dqkv, "sp", split_axis=1, concat_axis=3, tiled=True)
    qkv_grad = (
        qkv_back.reshape(tokens, 3, model_width)
        * jnp.array([query_scale, 1.0, 1.0], jnp.bfloat16)[:, None]
    )
    qkv_wide = qkv_grad.astype(jnp.float32)
    qkv_flat = qkv_grad.reshape(tokens, 3 * model_width)
    grad_self = tmatmul(flat_in, qkv_flat)
    grad_inputs = (grad_one + right_trans(qkv_flat, back_self)).reshape(inputs.shape)
    bias_grads = jnp.stack(
        [
            jnp.sum(qkv_wide[:, 0], axis=0),
            jnp.sum(qkv_wide[:, 2], axis=0),
            jnp.sum(grad_one, axis=0),
            jnp.sum(query_grad.astype(jnp.float32), axis=0),
            enc_value_sum,
            jnp.sum(grad_two, axis=0),
            jnp.sum(grad_three, axis=0),
            shift_one,
            shift_two,
            shift_three,
        ]
    )
    gain_grads = jnp.stack([gain_one, gain_two, gain_three])
    cells = model_width // (dp_count * sp_count)
    up_cells = grad_up_bias.shape[0] // (dp_count * sp_count)
    bias_split = bias_grads.reshape(10, dp_count, sp_count, cells)
    gain_split = gain_grads.reshape(3, dp_count, sp_count, cells)
    up_split = grad_up_bias.reshape(dp_count, sp_count, up_cells)
    sectioned = (
        lax.psum_scatter(
            grad_self.astype(jnp.bfloat16), "sp", scatter_dimension=1, tiled=True
        ).astype(jnp.float32),
        lax.psum_scatter(
            grad_self_out.astype(jnp.bfloat16), "sp", scatter_dimension=1, tiled=True
        ).astype(jnp.float32),
        lax.psum_scatter(
            grad_cross_q.astype(jnp.bfloat16), "sp", scatter_dimension=1, tiled=True
        ).astype(jnp.float32),
        lax.psum_scatter(
            grad_cross_kv.astype(jnp.bfloat16), "sp", scatter_dimension=1, tiled=True
        ).astype(jnp.float32),
        lax.psum_scatter(
            grad_cross_out.astype(jnp.bfloat16), "sp", scatter_dimension=1, tiled=True
        ).astype(jnp.float32),
        lax.psum_scatter(
            grad_up.astype(jnp.bfloat16), "sp", scatter_dimension=1, tiled=True
        ).astype(jnp.float32),
        lax.psum_scatter(
            grad_down.astype(jnp.bfloat16), "sp", scatter_dimension=1, tiled=True
        ).astype(jnp.float32),
        lax.psum_scatter(
            bias_split.astype(jnp.bfloat16), "sp", scatter_dimension=2, tiled=True
        ).astype(jnp.float32),
        lax.psum_scatter(
            gain_split.astype(jnp.bfloat16), "sp", scatter_dimension=2, tiled=True
        ).astype(jnp.float32),
        lax.psum_scatter(
            up_split.astype(jnp.bfloat16), "sp", scatter_dimension=1, tiled=True
        ).astype(jnp.float32),
    )
    reduced = (
        lax.psum_scatter(
            sectioned[0].astype(jnp.bfloat16), "dp", scatter_dimension=0, tiled=True
        ).astype(jnp.float32),
        lax.psum_scatter(
            sectioned[1].astype(jnp.bfloat16), "dp", scatter_dimension=0, tiled=True
        ).astype(jnp.float32),
        lax.psum_scatter(
            sectioned[2].astype(jnp.bfloat16), "dp", scatter_dimension=0, tiled=True
        ).astype(jnp.float32),
        lax.psum_scatter(
            sectioned[3].astype(jnp.bfloat16), "dp", scatter_dimension=0, tiled=True
        ).astype(jnp.float32),
        lax.psum_scatter(
            sectioned[4].astype(jnp.bfloat16), "dp", scatter_dimension=0, tiled=True
        ).astype(jnp.float32),
        lax.psum_scatter(
            sectioned[5].astype(jnp.bfloat16), "dp", scatter_dimension=0, tiled=True
        ).astype(jnp.float32),
        lax.psum_scatter(
            sectioned[6].astype(jnp.bfloat16), "dp", scatter_dimension=0, tiled=True
        ).astype(jnp.float32),
        lax.psum_scatter(
            sectioned[7].astype(jnp.bfloat16), "dp", scatter_dimension=1, tiled=True
        ).astype(jnp.float32),
        lax.psum_scatter(
            sectioned[8].astype(jnp.bfloat16), "dp", scatter_dimension=1, tiled=True
        ).astype(jnp.float32),
        lax.psum_scatter(
            sectioned[9].astype(jnp.bfloat16), "dp", scatter_dimension=0, tiled=True
        ).astype(jnp.float32),
    )
    return (
        output,
        grad_inputs,
        grad_encoder,
        reduced[0],
        reduced[1],
        reduced[2],
        reduced[3],
        reduced[4],
        reduced[5],
        reduced[6],
        reduced[7].reshape(10, cells),
        reduced[8].reshape(3, cells),
        reduced[9].reshape(up_cells),
    )


def solution(mesh):
    placed = (
        P("dp", "sp", None),
        P("dp", "sp", None),
        P("dp", "sp", None),
        P("dp", None),
        P("dp", None),
        P("dp", None),
        P("dp", None),
        P("dp", None),
        P("dp", None),
        P("dp", None),
        P(None, "dp"),
        P(None, "dp"),
        P("dp"),
        P("dp"),
    )
    return jax.shard_map(
        on_device,
        mesh=mesh,
        in_specs=placed,
        out_specs=(
            P("dp", "sp", None),
            P("dp", "sp", None),
            P("dp", "sp", None),
            P("dp", "sp"),
            P("dp", "sp"),
            P("dp", "sp"),
            P("dp", "sp"),
            P("dp", "sp"),
            P("dp", "sp"),
            P("dp", "sp"),
            P(None, ("dp", "sp")),
            P(None, ("dp", "sp")),
            P(("dp", "sp")),
        ),
        check_vma=False,
    )
```

profile of v0, /device:TPU:0, one launch (start us, length us, event | category | flops | bytes accessed | tf_op | source)
XLA Modules:
  0.0 1231.1 jit_solution(73304365855591040)
XLA Ops:
  19.4 18.9 %all-gather.8.cloned.1.call-done = bf16[512,1536]{1,0:T(8,128)(2,1)} async-done(((bf16[64,1536]{1,0:T(8,128)(2,1)}), bf16[512,1536]{1,0:T(8,128)(2,1)}) %all-gather.8.cloned.1.call-update) | async-done | bytes 1572880 | tf_op jit(solution)/shard_map/all_gather | solution.py:145
  52.6 47.1 %all-to-all-done = bf16[1,512,3,512]{1,2,0,3:T(4,128)(2,1)S(1)} async-done(((bf16[1,512,3,512]{1,2,0,3:T(4,128)(2,1)}), bf16[1,512,3,512]{1,2,0,3:T(4,128)(2,1)S(1)}, u32[]{:S(2)}, u32[]{:S(2)}) %all-to-all-start) | async-done | bytes 1572896 | tf_op jit(solution)/shard_map/all_to_all | solution.py:172
  105.9 42.2 %while.91 = (s32[]{:T(128)}, bf16[4,512,2,64]{1,3,2,0:T(8,128)(2,1)S(1)}, f32[4,2,512]{2,1,0:T(2,128)S(1)}, s32[4]{0:T(128)S(1)}, bf16[2048,2,64]{0,2,1:T(8,128)...) while((s32[]{:T(128)}, ...), condition=%wide.region_3.4_spmd, body=%wide.region_0.3_spmd.sunk | while | flops 556793344 | bytes 30838956 | solution.py:65
  256.5 37.6 %while.92 = (s32[]{:T(128)}, bf16[4,512,2,64]{1,3,2,0:T(8,128)(2,1)}, f32[4,2,512]{2,1,0:T(2,128)S(1)}, s32[]{:T(128)}, s32[4]{0:T(128)S(1)}, /*index=5*/bf16[20...) while((s32[]{:T(128)}, ...), condition=%wide.region_9.10_spmd, body=%wide.region_6.9_spmd.sunk | while | flops 555746304 | bytes 30843116 | solution.py:65
  303.0 13.3 %reduce.14 = bf16[2048,128]{1,0:T(8,128)(2,1)} reduce(bf16[2048,1,128]{2,1,0:T(2,128)(2,1)} %bitcast.357, bf16[]{:T(256)} %broadcast.262), dimensions={1}, to_apply=%bitcast.219.reduce_sub_computation | reduce | bytes 1048578
  382.2 15.1 %all-to-all-done.5 = bf16[4,2,32768]{2,1,0:T(2,128)(2,1)} async-done(((bf16[4,2,32768]{2,1,0:T(2,128)(2,1)}), bf16[4,2,32768]{2,1,0:T(2,128)(2,1)}, u32[]{:S(2)}, u32[]{:S(2)}) %all-to-all-start.5) | async-done | bytes 524320 | tf_op jit(solution)/shard_map/all_to_all | solution.py:303
  406.4 62.1 %while.93 = (s32[]{:T(128)}, f32[2048,2,64]{0,2,1:T(8,128)S(1)}, f32[2048,2,64]{0,2,1:T(8,128)S(1)}, bf16[4,512,2,64]{1,3,2,0:T(8,128)(2,1)}, s32[4]{0:T(128)S(1...) while((s32[]{:T(128)}, f32[2048,2,64]{0,2,1:T(8,128)S(1)}, ...), condition=%wide.region_20.21_spmd.clone, body=%wide.region_18.20_spmd.clone.sunk | while | flops 1368392704 | bytes 77893968 | solution.py:104
  491.3 18.4 %all_to_all.144 = bf16[4,2,32768]{2,1,0:T(2,128)(2,1)} all-to-all(bf16[4,2,32768]{2,1,0:T(2,128)(2,1)} %reshape.590), channel_id=1, replica_groups=mesh['dp'=8,'sp'=4] {'sp'}, dimensions={0} | all-to-all | bytes 1048576 | tf_op jit(solution)/shard_map/all_to_all | solution.py:334
  556.4 72.8 %while.94 = (s32[]{:T(128)}, f32[2048,2,64]{0,2,1:T(8,128)S(1)}, f32[2048,2,64]{0,2,1:T(8,128)}, bf16[4,512,2,64]{1,3,2,0:T(8,128)(2,1)}, s32[4]{0:T(128)S(1)}, ...) while((s32[]{:T(128)}, f32[2048,2,64]{0,2,1:T(8,128)S(1)}, ...), condition=%wide.region_25.26_spmd.clone, body=%wide.region_23.25_spmd.clone.sunk | while | flops 1369439744 | bytes 90472840 | solution.py:104
  655.5 41.4 %all-to-all-done.8 = bf16[1,2048,3,128]{3,2,0,1:T(4,128)(2,1)} async-done(((bf16[1,2048,3,128]{3,2,0,1:T(4,128)(2,1)}), bf16[1,2048,3,128]{3,2,0,1:T(4,128)(2,1)}, u32[]{:S(2)}, u32[]{:S(2)}) %all-to-all-start.8) | async-done | bytes 1572896 | tf_op jit(solution)/shard_map/all_to_all | solution.py:381
  756.0 26.4 %reduce-scatter.38.cloned.1.call-done = bf16[512,256]{0,1:T(8,128)(2,1)} async-done(((bf16[512,1024]{0,1:T(8,128)(2,1)}), bf16[512,256]{0,1:T(8,128)(2,1)}) %reduce-scatter.38.cloned.1.call-update) | async-done | bytes 262160 | tf_op jit(solution)/shard_map/reduce_scatter | solution.py:420
  784.3 42.8 %reduce-scatter.42.cloned.1.call-done = bf16[512,512]{1,0:T(8,128)(2,1)} async-done(((bf16[512,2048]{1,0:T(8,128)(2,1)}), bf16[512,512]{1,0:T(8,128)(2,1)}) %reduce-scatter.42.cloned.1.call-update) | async-done | bytes 524304 | tf_op jit(solution)/shard_map/reduce_scatter | solution.py:426
  839.3 24.4 %reduce-scatter.40.cloned.1.call-done = bf16[64,128]{1,0:T(8,128)(2,1)} async-done(((bf16[512,128]{1,0:T(8,128)(2,1)}), bf16[64,128]{1,0:T(8,128)(2,1)}) %reduce-scatter.40.cloned.1.call-update) | async-done | bytes 16400 | tf_op jit(solution)/shard_map/reduce_scatter | solution.py:455
  866.0 19.0 %reduce-scatter.64.cloned.1.call-done = bf16[3,8,1,16]{3,1,0,2:T(8,128)(2,1)} async-done(((bf16[3,8,4,16]{3,1,0,2:T(8,128)(2,1)}), bf16[3,8,1,16]{3,1,0,2:T(8,128)(2,1)}) %reduce-scatter.64.cloned.1.call-update) | async-done | bytes 784
  885.7 23.2 %all-reduce.5 = (bf16[3,8,1,16]{3,0,2,1:T(4,128)(2,1)S(1)}, bf16[8,1,64]{2,1,0:T(2,128)(2,1)S(1)}) all-reduce(bf16[3,8,1,16]{3,0,2,1:T(4,128)(2,1)S(1)} %copy.373, bf16[8,1,64]{2,1,0:T(2,128)(2,1)S(1)} %copy.375), channel_id=19, replica_groups=mesh['dp'=8,'sp'=4] {'dp'}, use_global_device_ids=true, to_apply=%region_56.57.clone | all-reduce | flops 896 | bytes 3584
  911.3 18.2 %reduce-scatter.62.cloned.1.call-done = bf16[128,2048]{1,0:T(8,128)(2,1)} async-done(((bf16[512,2048]{1,0:T(8,128)(2,1)}), bf16[128,2048]{1,0:T(8,128)(2,1)}) %reduce-scatter.62.cloned.1.call-update) | async-done | bytes 524304
  935.0 30.7 %reduce-scatter.34.cloned.1.call-done = bf16[64,128]{1,0:T(8,128)(2,1)} async-done(((bf16[512,128]{1,0:T(8,128)(2,1)}), bf16[64,128]{1,0:T(8,128)(2,1)}) %reduce-scatter.34.cloned.1.call-update) | async-done | bytes 16400 | tf_op jit(solution)/shard_map/reduce_scatter | solution.py:446
  967.0 35.8 %reduce-scatter.36.cloned.1.call-done = bf16[64,128]{1,0:T(8,128)(2,1)} async-done(((bf16[512,128]{1,0:T(8,128)(2,1)}), bf16[64,128]{1,0:T(8,128)(2,1)}) %reduce-scatter.36.cloned.1.call-update) | async-done | bytes 16400 | tf_op jit(solution)/shard_map/reduce_scatter | solution.py:449
  1005.6 34.7 %reduce-scatter.32.cloned.1.call-done = bf16[512,384]{0,1:T(8,128)(2,1)} async-done(((bf16[512,1536]{0,1:T(8,128)(2,1)}), bf16[512,384]{0,1:T(8,128)(2,1)}) %reduce-scatter.32.cloned.1.call-update) | async-done | bytes 393232 | tf_op jit(solution)/shard_map/reduce_scatter | solution.py:411
  1046.4 27.6 %reduce-scatter.50.cloned.1.call-done = bf16[10,1,1,16]{3,0,2,1:T(8,128)(2,1)} async-done(((bf16[10,8,1,16]{3,0,2,1:T(8,128)(2,1)}), bf16[10,1,1,16]{3,0,2,1:T(8,128)(2,1)}) %reduce-scatter.50.cloned.1.call-update) | async-done | bytes 336 | tf_op jit(solution)/shard_map/reduce_scatter | solution.py:464
  1075.2 35.5 %reduce-scatter.58.cloned.1.call-done = bf16[64,256]{1,0:T(8,128)(2,1)} async-done(((bf16[512,256]{1,0:T(8,128)(2,1)}), bf16[64,256]{1,0:T(8,128)(2,1)}) %reduce-scatter.58.cloned.1.call-update) | async-done | bytes 32784
  1112.4 35.6 %reduce-scatter.44.cloned.1.call-done = bf16[64,512]{1,0:T(8,128)(2,1)} async-done(((bf16[512,512]{1,0:T(8,128)(2,1)}), bf16[64,512]{1,0:T(8,128)(2,1)}) %reduce-scatter.44.cloned.1.call-update) | async-done | bytes 65552 | tf_op jit(solution)/shard_map/reduce_scatter | solution.py:458
  1149.5 35.9 %reduce-scatter.46.cloned.1.call-done = bf16[256,128]{1,0:T(8,128)(2,1)} async-done(((bf16[2048,128]{1,0:T(8,128)(2,1)}), bf16[256,128]{1,0:T(8,128)(2,1)}) %reduce-scatter.46.cloned.1.call-update) | async-done | bytes 65552 | tf_op jit(solution)/shard_map/reduce_scatter | solution.py:461
  1186.9 35.4 %reduce-scatter.52.cloned.1.call-done = bf16[64,384]{1,0:T(8,128)(2,1)} async-done(((bf16[512,384]{1,0:T(8,128)(2,1)}), bf16[64,384]{1,0:T(8,128)(2,1)}) %reduce-scatter.52.cloned.1.call-update) | async-done | bytes 49168
  (629 shorter events, 603.5 us)
Async XLA Ops:
  46.5 53.2 %all-to-all-start = ((bf16[1,512,3,512]{1,2,0,3:T(4,128)(2,1)}), bf16[1,512,3,512]{1,2,0,3:T(4,128)(2,1)S(1)}, u32[]{:S(2)}, u32[]{:S(2)}) async-start(bf16[1,512,3,512]{1,2,0,3:T(4,128)(2,1)} %copy.326), calls=%async_computation | async-start | bytes 4194304 | tf_op jit(solution)/shard_map/all_to_all | solution.py:172
  51.1 133.4 %all-gather.10.cloned.1.call-start = ((), (), s32[]{:S(2)}) async-start(), calls=%async_computation.28 | async-start | bytes 1179648 | tf_op jit(solution)/shard_map/all_gather | solution.py:148
  51.8 299.7 %all-gather.12.cloned.1.call-start = ((), (), s32[]{:S(2)}) async-start(), calls=%async_computation.29 | async-start | bytes 2359296 | tf_op jit(solution)/shard_map/all_gather | solution.py:150
  190.9 38.9 %all-to-all-start.3 = ((bf16[1,512,2,512]{1,2,0,3:T(2,128)(2,1)}), bf16[1,512,2,512]{1,2,0,3:T(2,128)(2,1)}, u32[]{:S(2)}, u32[]{:S(2)}) async-start(bf16[1,512,2,512]{1,2,0,3:T(2,128)(2,1)} %copy.339), calls=%async_computation.3 | async-start | bytes 2097152 | tf_op jit(solution)/shard_map/all_to_all | solution.py:179
  234.9 123.3 %all-gather.14.cloned.1.call-start = ((), (), s32[]{:S(2)}) async-start(), calls=%async_computation.30 | async-start | bytes 2359296 | tf_op jit(solution)/shard_map/all_gather | solution.py:151
  547.2 89.0 %all-to-all-start.9 = ((bf16[1,2048,2,128]{3,2,0,1:T(2,128)(2,1)}), bf16[1,2048,2,128]{3,2,0,1:T(2,128)(2,1)}, u32[]{:S(2)}, u32[]{:S(2)}) async-start(bf16[1,2048,2,128]{3,2,0,1:T(2,128)(2,1)} %copy.364), calls=%async_computation.9 | async-start | bytes 2097152 | tf_op jit(solution)/shard_map/all_to_all | solution.py:335
  636.2 60.7 %all-to-all-start.8 = ((bf16[1,2048,3,128]{3,2,0,1:T(4,128)(2,1)}), bf16[1,2048,3,128]{3,2,0,1:T(4,128)(2,1)}, u32[]{:S(2)}, u32[]{:S(2)}) async-start(bf16[1,2048,3,128]{3,2,0,1:T(4,128)(2,1)} %copy.360), calls=%async_computation.8 | async-start | bytes 4194304 | tf_op jit(solution)/shard_map/all_to_all | solution.py:381
  641.3 68.6 %reduce-scatter.60.cloned.1.call-start = ((), (), s32[]{:S(2)}) async-start(), calls=%async_computation.45 | async-start | bytes 655360
  646.0 75.2 %reduce-scatter.54.cloned.1.call-start = ((), (), s32[]{:S(2)}) async-start(), calls=%async_computation.42 | async-start | bytes 655360
  650.8 83.6 %reduce-scatter.56.cloned.1.call-start = ((), (), s32[]{:S(2)}) async-start(), calls=%async_computation.43 | async-start | bytes 655360
  653.3 101.3 %reduce-scatter.48.cloned.1.call-start = ((), (), s32[]{:S(2)}) async-start(), calls=%async_computation.39 | async-start | bytes 102400 | tf_op jit(solution)/shard_map/reduce_scatter | solution.py:432
  703.2 79.2 %reduce-scatter.38.cloned.1.call-start = ((), (), s32[]{:S(2)}) async-start(), calls=%async_computation.34 | async-start | bytes 1310720 | tf_op jit(solution)/shard_map/reduce_scatter | solution.py:420
  705.0 122.1 %reduce-scatter.42.cloned.1.call-start = ((), (), s32[]{:S(2)}) async-start(), calls=%async_computation.36 | async-start | bytes 2621440 | tf_op jit(solution)/shard_map/reduce_scatter | solution.py:426
  709.8 153.9 %reduce-scatter.40.cloned.1.call-start = ((), (), s32[]{:S(2)}) async-start(), calls=%async_computation.35 | async-start | bytes 147456 | tf_op jit(solution)/shard_map/reduce_scatter | solution.py:455
  711.5 173.5 %reduce-scatter.64.cloned.1.call-start = ((), (), s32[]{:S(2)}) async-start(), calls=%async_computation.47 | async-start | bytes 30720
  712.5 217.0 %reduce-scatter.62.cloned.1.call-start = ((), (), s32[]{:S(2)}) async-start(), calls=%async_computation.46 | async-start | bytes 2621440
  721.1 244.6 %reduce-scatter.34.cloned.1.call-start = ((), (), s32[]{:S(2)}) async-start(), calls=%async_computation.32 | async-start | bytes 147456 | tf_op jit(solution)/shard_map/reduce_scatter | solution.py:446
  722.9 279.8 %reduce-scatter.36.cloned.1.call-start = ((), (), s32[]{:S(2)}) async-start(), calls=%async_computation.33 | async-start | bytes 147456 | tf_op jit(solution)/shard_map/reduce_scatter | solution.py:449
  736.1 304.1 %reduce-scatter.32.cloned.1.call-start = ((), (), s32[]{:S(2)}) async-start(), calls=%async_computation.31 | async-start | bytes 1966080 | tf_op jit(solution)/shard_map/reduce_scatter | solution.py:411
  745.2 328.8 %reduce-scatter.50.cloned.1.call-start = ((), (), s32[]{:S(2)}) async-start(), calls=%async_computation.40 | async-start | bytes 36864 | tf_op jit(solution)/shard_map/reduce_scatter | solution.py:464
  756.0 354.8 %reduce-scatter.58.cloned.1.call-start = ((), (), s32[]{:S(2)}) async-start(), calls=%async_computation.44 | async-start | bytes 294912
  784.2 363.8 %reduce-scatter.44.cloned.1.call-start = ((), (), s32[]{:S(2)}) async-start(), calls=%async_computation.37 | async-start | bytes 589824 | tf_op jit(solution)/shard_map/reduce_scatter | solution.py:458
  827.1 358.3 %reduce-scatter.46.cloned.1.call-start = ((), (), s32[]{:S(2)}) async-start(), calls=%async_computation.38 | async-start | bytes 589824 | tf_op jit(solution)/shard_map/reduce_scatter | solution.py:461
  931.6 290.7 %reduce-scatter.52.cloned.1.call-start = ((), (), s32[]{:S(2)}) async-start(), calls=%async_computation.41 | async-start | bytes 442368
  (120 other events, 2303.2 us)
Sparse Core Ops, SparseCore 0:
  9.9 28.3 all-gather.7
  53.8 23.9 all-gather.9
  79.7 27.8 all-gather.11
  237.3 28.3 all-gather.13
  646.1 42.5 reduce-scatter.59
  690.8 21.2 reduce-scatter.53
  714.4 19.9 reduce-scatter.55
  737.2 17.3 reduce-scatter.47
  757.0 25.3 reduce-scatter.37
  784.5 42.5 reduce-scatter.41
  831.0 32.6 reduce-scatter.39
  866.4 18.6 reduce-scatter.63
  887.4 42.0 reduce-scatter.61
  932.9 32.6 reduce-scatter.33
  969.4 33.3 reduce-scatter.35
  1004.9 35.2 reduce-scatter.31
  1043.7 30.2 reduce-scatter.49
  1077.1 33.5 reduce-scatter.57
  1113.8 34.1 reduce-scatter.43
  1151.2 34.1 reduce-scatter.45
  1188.5 33.7 reduce-scatter.51
where the time goes:
time: 1240 us; the launch traced here: 1230 us
  waiting for transfers between devices  565 us (46%)
  matrix products  172 us (14%)
  local copies, waits for them, and re-layouts  169 us (14%)
  other arithmetic  125 us (10%)
  blocking collectives  109 us (9%)
  starting transfers between devices  42.3 us (3%)
  loops' own time  32.3 us (3%)
  between operations  15.8 us (1%)
    unnamed x28, waiting for transfers between devices  122 us
    unnamed x181, local copies, waits for them, and re-layouts  66.2 us
    unnamed x10, other arithmetic  51 us
    all_to_all x1, waiting for transfers between devices, on_device(): lax.all_to_all(self_proj.reshape(seq_local, tok_local, 3, model_width), '...  47.1 us
    reduce_scatter x1, waiting for transfers between devices, on_device(): lax.psum_scatter(grad_up.astype(jnp.bfloat16), 'sp', scatter_dimension=1,...  42.8 us
    all_to_all x1, waiting for transfers between devices, on_device(): lax.all_to_all(self_dqkv, 'sp', split_axis=1, concat_axis=3, tiled=True)  41.4 us
    reduce_scatter x1, waiting for transfers between devices, on_device(): lax.psum_scatter(sectioned[6].astype(jnp.bfloat16), 'dp', scatter_dimensi...  35.9 us
    reduce_scatter x1, waiting for transfers between devices, on_device(): lax.psum_scatter(sectioned[2].astype(jnp.bfloat16), 'dp', scatter_dimensi...  35.8 us
  transfers between devices with their start and end apart: 30, of which 21 were waited for; matrix products, arithmetic and copies ran while one was open for 27% of the time, Pallas kernels for 0%

commit v1 on v0

v1 whole, which is shorter than its diff:
```python
import functools

import jax
import jax.numpy as jnp
from jax import lax
from jax.experimental import pallas as pl
from jax.experimental.pallas import tpu as pltpu
from jax.sharding import PartitionSpec as P

H = 8
DH = 64
PAIR = 128

eps_norm = 1e-05
masked_out = -1e30
bf16 = jnp.bfloat16
f32 = jnp.float32
SCALE = DH ** (-0.5)

VMEM_LIMIT = 60 * 2**20


def nn(left, right):
    return lax.dot_general(left, right, (((1,), (0,)), ((), ())), preferred_element_type=f32)


def nt(left, right):
    return lax.dot_general(left, right, (((1,), (1,)), ((), ())), preferred_element_type=f32)


def tn(left, right):
    return lax.dot_general(left, right, (((0,), (0,)), ((), ())), preferred_element_type=f32)


def norm_stats(resid):
    centred = resid - jnp.mean(resid, axis=-1, keepdims=True)
    inv_std = lax.rsqrt(jnp.mean(centred * centred, axis=-1, keepdims=True) + eps_norm)
    return centred * inv_std, inv_std


def norm_backward(upstream, normed, inv_std, gain):
    scaled = upstream * gain
    centre_term = jnp.mean(scaled, axis=-1, keepdims=True)
    slope_term = jnp.mean(scaled * normed, axis=-1, keepdims=True)
    return inv_std * (scaled - centre_term - normed * slope_term)


def col_sum(value):
    return jnp.sum(value, axis=0, keepdims=True)


def chunk_of(d, block, n):
    even = d if d % 2 == 0 else 2 * n - 1 - d
    return even if block == 0 else 2 * n - 1 - even


def lane_head(rows, cols=PAIR):
    return lax.broadcasted_iota(jnp.int32, (rows, cols), 1) // DH


def one_head(pair_value, head):
    return jnp.where(lane_head(*pair_value.shape) == head, pair_value, jnp.zeros_like(pair_value))


def pair_slice(pair):
    return pl.ds(pl.multiple_of(pair * PAIR, PAIR), PAIR)


def write_blocks(out_ref, value, col0, n_dp, n_sp):
    rows = value.shape[0] // n_dp
    cols = value.shape[1] // n_sp
    low = value.astype(bf16)
    for i in range(n_dp):
        for j in range(n_sp):
            out_ref[i, j, :, col0 : col0 + cols] = low[
                i * rows : (i + 1) * rows, j * cols : (j + 1) * cols
            ]


def attend_rows(q_ref, k_ref, v_ref, att_ref, lse_ref, row0, rows, parts, pair):
    cols = pair_slice(pair)
    q2 = q_ref[row0 : row0 + rows, cols]
    both = []
    lse_now = lse_ref[row0 : row0 + rows, :]
    lane = lax.broadcasted_iota(jnp.int32, (rows, PAIR), 1)
    for h in range(2):
        qm = one_head(q2, h)
        scores = []
        for start, size, mask in parts:
            s = nt(qm, k_ref[start : start + size, cols])
            if mask is not None:
                s = jnp.where(mask(rows, size), s, masked_out)
            scores.append(s)
        top = functools.reduce(
            jnp.maximum, [jnp.max(s, axis=-1, keepdims=True) for s in scores]
        )
        total = 0.0
        result = 0.0
        for s, (start, size, _) in zip(scores, parts):
            e = jnp.exp(s - top)
            total = total + jnp.sum(e, axis=-1, keepdims=True)
            result = result + nn(e.astype(bf16), v_ref[start : start + size, cols])
        both.append(result / total)
        lse_now = jnp.where(lane == pair * 2 + h, top + jnp.log(total), lse_now)
    lse_ref[row0 : row0 + rows, :] = lse_now
    att_ref[row0 : row0 + rows, cols] = jnp.where(
        lane_head(rows) == 0, both[0], both[1]
    ).astype(bf16)


def attend_rows_back(
    q_ref, k_ref, v_ref, att_ref, g_ref, lse_ref, qt_ref, gt_ref,
    dq_ref, dkt_ref, dvt_ref, row0, rows, parts, pair,
):
    cols = pair_slice(pair)
    q2 = q_ref[row0 : row0 + rows, cols]
    g2 = g_ref[row0 : row0 + rows, cols]
    prod = g2.astype(f32) * att_ref[row0 : row0 + rows, cols].astype(f32)
    lse_all = lse_ref[row0 : row0 + rows, :]
    lane = lax.broadcasted_iota(jnp.int32, (rows, PAIR), 1)
    both = []
    for h in range(2):
        head = pair * 2 + h
        hrows = pl.ds(pl.multiple_of(head * DH, DH), DH)
        qm = one_head(q2, h)
        gm = one_head(g2, h)
        qt = qt_ref[hrows, row0 : row0 + rows]
        gt = gt_ref[hrows, row0 : row0 + rows]
        lse = jnp.sum(jnp.where(lane == head, lse_all, 0.0), axis=-1, keepdims=True)
        delta = jnp.sum(jnp.where(lane // DH == h, prod, 0.0), axis=-1, keepdims=True)
        dq = 0.0
        for start, size, mask, adds in parts:
            k2 = k_ref[start : start + size, cols]
            v2 = v_ref[start : start + size, cols]
            p = jnp.exp(nt(qm, k2) - lse)
            if mask is not None:
                p = jnp.where(mask(rows, size), p, 0.0)
            ds = (p * (nt(gm, v2) - delta)).astype(bf16)
            dq = dq + nn(ds, k2)
            dk = nn(qt, ds)
            dv = nn(gt, p.astype(bf16))
            if adds:
                dk = dk + dkt_ref[hrows, start : start + size]
                dv = dv + dvt_ref[hrows, start : start + size]
            dkt_ref[hrows, start : start + size] = dk
            dvt_ref[hrows, start : start + size] = dv
        both.append(dq)
    dq_ref[row0 : row0 + rows, cols] = (
        jnp.where(lane_head(rows) == 0, both[0], both[1]).astype(bf16)
    )


def diagonal(rows, size):
    row = lax.broadcasted_iota(jnp.int32, (rows, size), 0)
    col = lax.broadcasted_iota(jnp.int32, (rows, size), 1)
    return col <= row


def causal_parts(chunk, size):
    parts = []
    if chunk:
        parts.append((0, chunk * size, None))
    parts.append((chunk * size, size, diagonal))
    return parts


def self_forward_kernel(n, d_ref, x_ref, w_ref, vec_ref, q_ref, k_ref, v_ref, att_ref, lse_ref):
    length, width = x_ref.shape
    rows = q_ref.shape[0]
    size = rows // 2
    d = d_ref[0]
    step = min(512, length)

    def project(i, carry):
        here = pl.ds(pl.multiple_of(i * step, step), step)
        kv = nn(x_ref[here, :], w_ref[:, width : 3 * width])
        k_ref[here, :] = kv[:, :width].astype(bf16)
        v_ref[here, :] = (kv[:, width:] + vec_ref[1:2, :]).astype(bf16)
        return carry

    lax.fori_loop(0, length // step, project, 0)
    even = jnp.where(d % 2 == 0, d, 2 * n - 1 - d)
    for block in range(2):
        chunk = even if block == 0 else 2 * n - 1 - even
        xb = x_ref[pl.ds(pl.multiple_of(chunk * size, size), size), :]
        q_ref[block * size : (block + 1) * size, :] = (
            (nn(xb, w_ref[:, :width]) + vec_ref[0:1, :]) * SCALE
        ).astype(bf16)
    lse_ref[...] = jnp.zeros_like(lse_ref)

    for which in range(n):

        @pl.when(d == which)
        def _(which=which):
            def pairs(pair, carry):
                for block in range(2):
                    chunk = chunk_of(which, block, n)
                    attend_rows(
                        q_ref, k_ref, v_ref, att_ref, lse_ref, block * size, size,
                        causal_parts(chunk, size), pair,
                    )
                return carry

            lax.fori_loop(0, H // 2, pairs, 0)


def cross_forward_kernel(
    n, d_ref, lim_ref, att_ref, x_ref, enc_ref, wso_ref, wcq_ref, wckv_ref, vec_ref,
    res_ref, cq_ref, ek_ref, ev_ref, catt_ref, clse_ref,
):
    length, width = enc_ref.shape
    rows = att_ref.shape[0]
    size = rows // 2
    d = d_ref[0]
    limit = lim_ref[0]
    even = jnp.where(d % 2 == 0, d, 2 * n - 1 - d)
    for block in range(2):
        chunk = even if block == 0 else 2 * n - 1 - even
        here = slice(block * size, (block + 1) * size)
        xb = x_ref[pl.ds(pl.multiple_of(chunk * size, size), size), :].astype(f32)
        res_ref[here, :] = xb + nn(att_ref[here, :], wso_ref[...]) + vec_ref[2:3, :]
    normed, _ = norm_stats(res_ref[...])
    hidden = (normed * vec_ref[10:11, :] + vec_ref[7:8, :]).astype(bf16)
    cq_ref[...] = ((nn(hidden, wcq_ref[...]) + vec_ref[3:4, :]) * SCALE).astype(bf16)
    step = min(512, length)

    def project(i, carry):
        here = pl.ds(pl.multiple_of(i * step, step), step)
        kv = nn(enc_ref[here, :], wckv_ref[...])
        ek_ref[here, :] = kv[:, :width].astype(bf16)
        ev_ref[here, :] = (kv[:, width:] + vec_ref[4:5, :]).astype(bf16)
        return carry

    lax.fori_loop(0, length // step, project, 0)
    clse_ref[...] = jnp.zeros_like(clse_ref)

    def visible(count, keys):
        return lax.broadcasted_iota(jnp.int32, (count, keys), 1) < limit

    def pairs(pair, carry):
        for block in range(2):
            attend_rows(
                cq_ref, ek_ref, ev_ref, catt_ref, clse_ref, block * size, size,
                [(0, length, visible)], pair,
            )
        return carry

    lax.fori_loop(0, H // 2, pairs, 0)


def feed_forward_kernel(
    n_dp, n_sp, res1_ref, catt_ref, wco_ref, wup_ref, wdn_ref, vec_ref, upb_ref, cot0_ref, cot1_ref,
    out0_ref, out1_ref, gtwo_ref, cgrad_ref, gw_ref, upsum_ref, small_ref,
    up_scr, act_scr, upl_scr,
):
    rows, width = res1_ref.shape
    size = rows // 2
    hidden_units = wup_ref.shape[1]
    step = min(512, hidden_units)
    blocks = hidden_units // step
    normed, _ = norm_stats(res1_ref[...])
    hidden_one = normed * vec_ref[10:11, :] + vec_ref[7:8, :]
    res2 = hidden_one + nn(catt_ref[...], wco_ref[...]) + vec_ref[5:6, :]
    normed2, inv2 = norm_stats(res2)
    hidden_two = normed2 * vec_ref[11:12, :] + vec_ref[8:9, :]
    h2_low = hidden_two.astype(bf16)
    down = jnp.zeros((rows, width), f32)
    for b in range(blocks):
        cols = slice(b * step, (b + 1) * step)
        up = nn(h2_low, wup_ref[:, cols]) + upb_ref[0:1, cols]
        up_scr[:, cols] = up
        act = (up * jax.nn.sigmoid(up)).astype(bf16)
        act_scr[:, cols] = act
        down = down + nn(act, wdn_ref[cols, :])
    res3 = hidden_two + down + vec_ref[6:7, :]
    normed3, inv3 = norm_stats(res3)
    result = (normed3 * vec_ref[12:13, :] + vec_ref[9:10, :]).astype(bf16)
    out0_ref[...] = result[:size]
    out1_ref[...] = result[size:]
    upstream = jnp.concatenate([cot0_ref[...], cot1_ref[...]], axis=0).astype(f32)
    small_ref[...] = jnp.zeros_like(small_ref)
    small_ref[12:13, :] = col_sum(upstream * normed3)
    small_ref[9:10, :] = col_sum(upstream)
    grad_three = norm_backward(upstream, normed3, inv3, vec_ref[12:13, :])
    small_ref[6:7, :] = col_sum(grad_three)
    down_low = grad_three.astype(bf16)
    h2_t = h2_low.T
    grad_h2 = grad_three
    part_rows = hidden_units // n_dp
    own_rows = width // n_dp
    groups = part_rows // own_rows
    piece = width // n_sp
    up_piece = hidden_units // n_sp
    for b in range(blocks):
        cols = slice(b * step, (b + 1) * step)
        gdown = tn(act_scr[:, cols], down_low).astype(bf16)
        for r in range(step // own_rows):
            at = b * step + r * own_rows
            i, g = at // part_rows, (at % part_rows) // own_rows
            for j in range(n_sp):
                base = piece + up_piece + g * piece
                gw_ref[i, j, :, base : base + piece] = gdown[
                    r * own_rows : (r + 1) * own_rows, j * piece : (j + 1) * piece
                ]
        up = up_scr[:, cols]
        sig = jax.nn.sigmoid(up)
        up_low = (
            nt(down_low, wdn_ref[cols, :]) * sig * (1.0 + up * (1.0 - sig))
        ).astype(bf16)
        upl_scr[:, cols] = up_low
        upsum_ref[0:1, cols] = col_sum(up_low.astype(f32))
        grad_h2 = grad_h2 + nt(up_low, wup_ref[:, cols])
    for j in range(n_sp):
        cols = slice(j * up_piece, (j + 1) * up_piece)
        gup = nn(h2_t, upl_scr[:, cols]).astype(bf16)
        for i in range(n_dp):
            gw_ref[i, j, :, piece : piece + up_piece] = gup[i * own_rows : (i + 1) * own_rows, :]
    small_ref[11:12, :] = col_sum(grad_h2 * normed2)
    small_ref[8:9, :] = col_sum(grad_h2)
    grad_two = norm_backward(grad_h2, normed2, inv2, vec_ref[11:12, :])
    small_ref[5:6, :] = col_sum(grad_two)
    gtwo_ref[...] = grad_two
    two_low = grad_two.astype(bf16)
    write_blocks(gw_ref, tn(catt_ref[...], two_low), 0, n_dp, n_sp)
    cgrad_ref[...] = nt(two_low, wco_ref[...]).astype(bf16)


def ones_sum(t_ref):
    return nt(jnp.ones((8, t_ref.shape[1]), bf16), t_ref[...])[0:1, :]


def cross_backward_kernel(
    n_dp, n_sp, lim_ref, cq_ref, ek_ref, ev_ref, catt_ref, cgrad_ref, clse_ref, enc_ref, wcq_ref, wckv_ref,
    wso_ref, vec_ref, res1_ref, att_ref, gtwo_ref, small_in_ref,
    genc_ref, gone_ref, sgrad_ref, gw_ref, small_ref,
    qt_scr, gt_scr, dq_scr, dkt_scr, dvt_scr, low_scr,
):
    length, width = enc_ref.shape
    rows = cq_ref.shape[0]
    size = rows // 2
    limit = lim_ref[0]
    qt_scr[...] = cq_ref[...].T
    gt_scr[...] = cgrad_ref[...].T
    half = length // 2

    def pairs(pair, carry):
        for block in range(2):
            parts = []
            for part in range(2):
                start = part * half

                def visible(count, keys, start=start):
                    return lax.broadcasted_iota(jnp.int32, (count, keys), 1) + start < limit

                parts.append((start, half, visible, block == 1))
            attend_rows_back(
                cq_ref, ek_ref, ev_ref, catt_ref, cgrad_ref, clse_ref, qt_scr, gt_scr,
                dq_scr, dkt_scr, dvt_scr, block * size, size, parts, pair,
            )
        return carry

    lax.fori_loop(0, H // 2, pairs, 0)
    low_scr[:width, :] = dkt_scr[...].astype(bf16)
    low_scr[width:, :] = dvt_scr[...].astype(bf16)
    query_grad = (dq_scr[...].astype(f32) * SCALE).astype(bf16)
    small_ref[...] = small_in_ref[...]
    small_ref[3:4, :] = col_sum(query_grad.astype(f32))
    small_ref[4:5, :] = ones_sum(low_scr.at[width:, :])
    normed, inv = norm_stats(res1_ref[...])
    hidden = (normed * vec_ref[10:11, :] + vec_ref[7:8, :]).astype(bf16)
    piece = width // n_sp
    write_blocks(gw_ref, tn(hidden, query_grad), 0, n_dp, n_sp)
    grad_h1 = gtwo_ref[...] + nt(query_grad, wcq_ref[...])
    small_ref[10:11, :] = col_sum(grad_h1 * normed)
    small_ref[7:8, :] = col_sum(grad_h1)
    grad_one = norm_backward(grad_h1, normed, inv, vec_ref[10:11, :])
    small_ref[2:3, :] = col_sum(grad_one)
    gone_ref[...] = grad_one
    one_low = grad_one.astype(bf16)
    write_blocks(gw_ref, tn(att_ref[...], one_low), 3 * piece, n_dp, n_sp)
    sgrad_ref[...] = nt(one_low, wso_ref[...]).astype(bf16)
    write_blocks(gw_ref, nn(low_scr[...], enc_ref[...]).T, piece, n_dp, n_sp)
    step = min(512, length)

    def back(i, carry):
        here = pl.ds(pl.multiple_of(i * step, step), step)
        genc_ref[here, :] = nn(wckv_ref[...], low_scr[:, here]).T.astype(bf16)
        return carry

    lax.fori_loop(0, length // step, back, 0)


def self_backward_kernel(
    n, n_dp, n_sp, d_ref, q_ref, k_ref, v_ref, att_ref, sgrad_ref, lse_ref, x_ref, w_ref, gone_ref, small_in_ref,
    gin_ref, gw_ref, small_ref,
    qt_scr, gt_scr, dq_scr, dkt_scr, dvt_scr, low_scr,
):
    length, width = x_ref.shape
    rows = q_ref.shape[0]
    size = rows // 2
    d = d_ref[0]
    qt_scr[...] = q_ref[...].T
    gt_scr[...] = sgrad_ref[...].T
    for which in range(n):

        @pl.when(d == which)
        def _(which=which):
            order = sorted(range(2), key=lambda block: -chunk_of(which, block, n))
            top = chunk_of(which, order[0], n)
            if top + 1 < 2 * n:
                rest = (2 * n - 1 - top) * size
                dkt_scr[:, (top + 1) * size :] = jnp.zeros((width, rest), f32)
                dvt_scr[:, (top + 1) * size :] = jnp.zeros((width, rest), f32)

            def pairs(pair, carry):
                for place, block in enumerate(order):
                    chunk = chunk_of(which, block, n)
                    parts = []
                    for start, count, mask in causal_parts(chunk, size):
                        while count > 4 * size:
                            parts.append((start, 4 * size, mask, place == 1))
                            start, count = start + 4 * size, count - 4 * size
                        parts.append((start, count, mask, place == 1))
                    attend_rows_back(
                        q_ref, k_ref, v_ref, att_ref, sgrad_ref, lse_ref, qt_scr, gt_scr,
                        dq_scr, dkt_scr, dvt_scr, block * size, size, parts, pair,
                    )
                return carry

            lax.fori_loop(0, H // 2, pairs, 0)

    low_scr[:width, :] = dkt_scr[...].astype(bf16)
    low_scr[width:, :] = dvt_scr[...].astype(bf16)
    q_grad = (dq_scr[...].astype(f32) * SCALE).astype(bf16)
    small_ref[...] = small_in_ref[...]
    small_ref[0:1, :] = col_sum(q_grad.astype(f32))
    small_ref[1:2, :] = ones_sum(low_scr.at[width:, :])
    kv_grad = nn(low_scr[...], x_ref[...]).T
    even = jnp.where(d % 2 == 0, d, 2 * n - 1 - d)
    step = min(512, length)

    def back(i, carry):
        here = pl.ds(pl.multiple_of(i * step, step), step)
        gin_ref[here, :] = nn(w_ref[:, width:], low_scr[:, here]).T.astype(bf16)
        return carry

    lax.fori_loop(0, length // step, back, 0)
    wq_grad = jnp.zeros((width, width), f32)
    for block in range(2):
        chunk = even if block == 0 else 2 * n - 1 - even
        here = pl.ds(pl.multiple_of(chunk * size, size), size)
        own = slice(block * size, (block + 1) * size)
        wq_grad = wq_grad + tn(x_ref[here, :], q_grad[own])
        gin_ref[here, :] = (
            gin_ref[here, :].astype(f32)
            + gone_ref[own, :]
            + nt(q_grad[own], w_ref[:, :width])
        ).astype(bf16)
    grads = jnp.concatenate([wq_grad, kv_grad], axis=1)
    write_blocks(gw_ref, grads, 0, n_dp, n_sp)


def run_kernel(kernel, outs, args, scratch=(), scalars=0, flops=0):
    whole = pl.BlockSpec(memory_space=pltpu.VMEM)
    scalar = pl.BlockSpec(memory_space=pltpu.SMEM)
    return pl.pallas_call(
        kernel,
        out_shape=tuple(jax.ShapeDtypeStruct(shape, kind) for shape, kind in outs),
        in_specs=[scalar] * scalars + [whole] * (len(args) - scalars),
        out_specs=tuple(whole for _ in outs),
        scratch_shapes=list(scratch),
        compiler_params=pltpu.CompilerParams(vmem_limit_bytes=VMEM_LIMIT),
        cost_estimate=pl.CostEstimate(flops=flops, bytes_accessed=10 * 2**20, transcendentals=0),
    )(*args)


def zigzag_pairs(n):
    def place(chunk):
        return chunk if chunk < n else 2 * n - 1 - chunk

    evens = [(i, place(2 * i)) for i in range(n)]
    odds = [(i, place(2 * i + 1)) for i in range(n)]
    return evens, odds


def on_device(
    inputs, encoder, cotangent, w_self, w_self_out, w_cross_q, w_cross_kv, w_cross_out, w_up, w_down,
    biases, norm_gains, up_bias, source_lengths,
):
    n = lax.axis_size("sp")
    n_dp = lax.axis_size("dp")
    _, rows, width = inputs.shape
    size = rows // 2
    length = n * rows
    hidden_units = w_up.shape[1]
    own = w_self.shape[0]
    d = lax.axis_index("sp").astype(jnp.int32).reshape(1)
    limit = source_lengths.astype(jnp.int32)

    groups = up_bias.shape[0] // own
    first = jnp.concatenate(
        [w_self, biases.T, norm_gains.T, up_bias.reshape(groups, own).T,
         jnp.zeros((own, PAIR - 13 - groups), bf16)], axis=1,
    )
    first = lax.all_gather(first, "dp", axis=0, tiled=True)
    x_full = lax.all_gather(inputs[0], "sp", axis=0, tiled=True)
    rest = jnp.concatenate([w_cross_kv, w_self_out, w_cross_q, w_cross_out, w_up], axis=1)
    rest = lax.all_gather(rest, "dp", axis=0, tiled=True)
    full_down = lax.all_gather(w_down, "dp", axis=0, tiled=True)
    enc_full = lax.all_gather(encoder[0], "sp", axis=0, tiled=True)
    evens, odds = zigzag_pairs(n)
    cot0 = lax.ppermute(cotangent[0, :size], "sp", evens)
    cot1 = lax.ppermute(cotangent[0, size:], "sp", odds)

    full_self = first[:, : 3 * width]
    vec = first[:, 3 * width :].T.astype(f32)
    upb = (
        vec[13 : 13 + groups].reshape(groups, n_dp, own).transpose(1, 0, 2).reshape(1, hidden_units)
    )
    wckv = rest[:, : 2 * width]
    wso = rest[:, 2 * width : 3 * width]
    wcq = rest[:, 3 * width : 4 * width]
    wco = rest[:, 4 * width : 5 * width]
    wup = rest[:, 5 * width :]

    q, k, v, att, lse = run_kernel(
        functools.partial(self_forward_kernel, n),
        [((rows, width), bf16), ((length, width), bf16), ((length, width), bf16),
         ((rows, width), bf16), ((rows, PAIR), f32)],
        (d, x_full, full_self, vec), scalars=1, flops=6 * 10**9,
    )
    res1, cq, ek, ev, catt, clse = run_kernel(
        functools.partial(cross_forward_kernel, n),
        [((rows, width), f32), ((rows, width), bf16), ((length, width), bf16),
         ((length, width), bf16), ((rows, width), bf16), ((rows, PAIR), f32)],
        (d, limit, att, x_full, enc_full, wso, wcq, wckv, vec), scalars=2, flops=12 * 10**9,
    )
    piece = width // n
    up_piece = hidden_units // n
    out0, out1, gtwo, cgrad, gw1, upsum, small = run_kernel(
        functools.partial(feed_forward_kernel, n_dp, n),
        [((size, width), bf16), ((size, width), bf16), ((rows, width), f32), ((rows, width), bf16),
         ((n_dp, n, own, piece + up_piece + groups * piece), bf16), ((8, hidden_units), f32),
         ((16, width), f32)],
        (res1, catt, wco, wup, full_down, vec, upb, cot0, cot1),
        scratch=[pltpu.VMEM((rows, hidden_units), f32), pltpu.VMEM((rows, hidden_units), bf16),
                 pltpu.VMEM((rows, hidden_units), bf16)],
        flops=8 * 10**9,
    )
    back_scratch = [
        pltpu.VMEM((width, rows), bf16), pltpu.VMEM((width, rows), bf16), pltpu.VMEM((rows, width), bf16),
        pltpu.VMEM((width, length), f32), pltpu.VMEM((width, length), f32),
        pltpu.VMEM((2 * width, length), bf16),
    ]
    genc, gone, sgrad, gw2, small = run_kernel(
        functools.partial(cross_backward_kernel, n_dp, n),
        [((length, width), bf16), ((rows, width), f32), ((rows, width), bf16),
         ((n_dp, n, own, 4 * piece), bf16), ((16, width), f32)],
        (limit, cq, ek, ev, catt, cgrad, clse, enc_full, wcq, wckv, wso, vec, res1, att, gtwo, small),
        scratch=back_scratch, scalars=1, flops=24 * 10**9,
    )
    gin, gw3, small = run_kernel(
        functools.partial(self_backward_kernel, n, n_dp, n),
        [((length, width), bf16), ((n_dp, n, own, 3 * piece), bf16), ((16, width), f32)],
        (d, q, k, v, att, sgrad, lse, x_full, full_self, gone, small),
        scratch=back_scratch, scalars=1, flops=16 * 10**9,
    )

    back0 = [(b, a) for a, b in evens]
    back1 = [(b, a) for a, b in odds]
    output = jnp.concatenate(
        [lax.ppermute(out0, "sp", back0), lax.ppermute(out1, "sp", back1)], axis=0
    )[None]
    grad_encoder = lax.psum_scatter(genc, "sp", scatter_dimension=0, tiled=True).astype(f32)[None]
    grad_inputs = lax.psum_scatter(gin, "sp", scatter_dimension=0, tiled=True).astype(f32)[None]

    def reduce_blocks(blocks):
        part = lax.psum_scatter(blocks, "dp", scatter_dimension=0)
        return lax.psum_scatter(part, "sp", scatter_dimension=0).astype(f32)

    one, two, three = reduce_blocks(gw1), reduce_blocks(gw2), reduce_blocks(gw3)
    cells = width // (n_dp * n)
    up_cells = hidden_units // (n_dp * n)
    tiny = jnp.concatenate(
        [small[:13].reshape(13, n_dp, n, cells).transpose(1, 2, 0, 3).reshape(n_dp, n, 13 * cells),
         upsum[0].reshape(n_dp, n, up_cells)], axis=-1,
    )
    tiny = reduce_blocks(tiny.astype(bf16))
    grad_rows = tiny[: 13 * cells].reshape(13, cells)
    return (
        output,
        grad_inputs,
        grad_encoder,
        three_split(three, piece, 0),
        two[:, 3 * piece :],
        two[:, :piece],
        two[:, piece : 3 * piece],
        one[:, :piece],
        one[:, piece : piece + up_piece],
        one[:, piece + up_piece :].reshape(own, groups, piece).transpose(1, 0, 2).reshape(groups * own, piece),
        grad_rows[:10],
        grad_rows[10:],
        tiny[13 * cells :],
    )


def three_split(blocks, piece, start):
    return blocks[:, start : start + 3 * piece]


def solution(mesh):
    weight = P("dp", None)
    tokens = P("dp", "sp", None)
    return jax.shard_map(
        on_device,
        mesh=mesh,
        in_specs=(tokens,) * 3 + (weight,) * 7 + (P(None, "dp"), P(None, "dp"), P("dp"), P("dp")),
        out_specs=(tokens,) * 3
        + (P("dp", "sp"),) * 7
        + (P(None, ("dp", "sp")), P(None, ("dp", "sp")), P(("dp", "sp"))),
        check_vma=False,
    )
```

time: 1240 us -> 605 us (0.49)
  waiting for transfers between devices: 565 us -> 371 us
  matrix products: 172 us -> 0 us
  local copies, waits for them, and re-layouts: 169 us -> 27.5 us
  Pallas kernels: 0 us -> 121 us
  other arithmetic: 125 us -> 11.4 us
  blocking collectives: 109 us -> 33.8 us
  loops' own time: 32.3 us -> 0 us
  starting transfers between devices: 42.3 us -> 16.6 us
    dot_general x77 -> x0, matrix products: 172 us -> none  [the longest x16 32.3 us: one_block(): jnp.einsum('qhe,khe->hqk', query_block, key_rows, preferred_element_type=...]
    pallas_call x0 -> x5, Pallas kernels: none -> 121 us  [run_kernel(): pl.pallas_call(kernel, out_shape=tuple((jax.ShapeDtypeStruct(shape, kind)...]
    all_to_all x9 -> x0, waiting for transfers between devices: 121 us -> none  [the longest x1 47.1 us: on_device(): lax.all_to_all(self_proj.reshape(seq_local, tok_local, 3, model_width), '...]
    unnamed x28 -> x13, waiting for transfers between devices: 122 us -> 4.39 us
    all_gather x4 -> x5, waiting for transfers between devices: 19 us -> 124 us  [the longest x1 43.4 us: on_device(): x_full = lax.all_gather(inputs[0], 'sp', axis=0, tiled=True)]
    reduce_scatter x10 -> x8, waiting for transfers between devices: 303 us -> 243 us  [the longest x3 95.2 us: reduce_blocks(): part = lax.psum_scatter(blocks, 'dp', scatter_dimension=0)]
    unnamed x181 -> x30, local copies, waits for them, and re-layouts: 66.2 us -> 7.05 us
    all_gather x6 -> x0, blocking collectives: 57.4 us -> none  [the longest x1 11 us: on_device(): lax.all_gather(w_cross_out, 'dp', axis=0, tiled=True)]
  transfers between devices with their start and end apart: 30 -> 17, of which waited for: 21 -> 13; matrix products, arithmetic and copies ran while one was open for 27% -> 5% of each run, Pallas kernels for 0% -> 7%
where the time goes in v1:
time: 605 us; the launch traced here: 597 us
  waiting for transfers between devices  371 us (61%)
  Pallas kernels  121 us (20%)
  blocking collectives  33.8 us (6%)
  local copies, waits for them, and re-layouts  27.5 us (5%)
  starting transfers between devices  16.6 us (3%)
  between operations  15.3 us (3%)
  other arithmetic  11.4 us (2%)
    pallas_call x5, Pallas kernels, run_kernel(): pl.pallas_call(kernel, out_shape=tuple((jax.ShapeDtypeStruct(shape, kind)...  121 us
    reduce_scatter x3, waiting for transfers between devices, reduce_blocks(): part = lax.psum_scatter(blocks, 'dp', scatter_dimension=0)  95.2 us
    reduce_scatter x3, waiting for transfers between devices, reduce_blocks(): return lax.psum_scatter(part, 'sp', scatter_dimension=0).astype(f32)  61.8 us
    all_gather x1, waiting for transfers between devices, on_device(): x_full = lax.all_gather(inputs[0], 'sp', axis=0, tiled=True)  43.4 us
    reduce_scatter x1, waiting for transfers between devices, on_device(): lax.psum_scatter(genc, 'sp', scatter_dimension=0, tiled=True).astype(f32)  43.3 us
    all_gather x1, waiting for transfers between devices, on_device(): enc_full = lax.all_gather(encoder[0], 'sp', axis=0, tiled=True)  42.6 us
    reduce_scatter x1, waiting for transfers between devices, on_device(): lax.psum_scatter(gin, 'sp', scatter_dimension=0, tiled=True).astype(f32)  42.3 us
    unnamed x2, blocking collectives  33.8 us
  transfers between devices with their start and end apart: 17, of which 13 were waited for; matrix products, arithmetic and copies ran while one was open for 5% of the time, Pallas kernels for 7%

profile of v1, /device:TPU:0, one launch (start us, length us, event | category | flops | bytes accessed | tf_op | source)
XLA Modules:
  0.0 596.6 jit_solution(14243091132525705415)
XLA Ops:
  18.5 7.7 %collective-permute-start.1 = (bf16[256,512]{1,0:T(8,128)(2,1)S(1)}, bf16[256,512]{1,0:T(8,128)(2,1)S(1)}, u32[]{:S(2)}, u32[]{:S(2)}) collective-permute-start(bf16[256,512]{1,0:T(8,128)(2,1)S(1)} %get-tuple-element.68), channel_id=1, source_target_pairs={{0,1},{1,3},{2,2},{3,0},{4,5},{5,7},{6,6},{7,4},{8,9},{9,11},{10,1... | collective-permute-start | bytes 786440 | tf_op jit(solution)/shard_map/ppermute | solution.py:513
  26.9 13.6 %all-gather.8.cloned.1.call-done = bf16[512,1664]{1,0:T(8,128)(2,1)} async-done(((bf16[64,1664]{1,0:T(8,128)(2,1)}), bf16[512,1664]{1,0:T(8,128)(2,1)}) %all-gather.8.cloned.1.call-update) | async-done | bytes 1703952 | tf_op jit(solution)/shard_map/all_gather | solution.py:505
  44.7 43.4 %all-gather.14.cloned.1.call-done = bf16[1,2048,512]{2,1,0:T(8,128)(2,1)} async-done(((bf16[1,512,512]{2,1,0:T(8,128)(2,1)}), bf16[1,2048,512]{2,1,0:T(8,128)(2,1)}) %all-gather.14.cloned.1.call-update) | async-done | bytes 2097168 | tf_op jit(solution)/shard_map/all_gather | solution.py:506
  88.1 18.3 %shard_map.237 = (bf16[512,512]{1,0:T(8,128)(2,1)}, bf16[2048,512]{1,0:T(8,128)(2,1)}, bf16[2048,512]{1,0:T(8,128)(2,1)}, bf16[512,512]{1,0:T(8,128)(2,1)}, f32[512,128]{1,0:T(8,128)}) custom-call(s32[1]{0:T(128)} %bitcast.d_ref, bf16[2048,512]{1,0:T(8,128)(2,1)} %bitcast.61, bf16[512,1536]{1,0:T(8,128)(2,1)} %slice.118.w_ref, f32[128,512]{1,0:T(8,128)} %copy.61.vec_ref), custom_call_target="tpu_custom_call" | custom-call | flops 6000000000 | bytes 10485760 | tf_op jit(solution)/shard_map/pallas_call | solution.py:466
  106.4 21.8 %all-gather.10.cloned.1.call-done = bf16[512,4608]{1,0:T(8,128)(2,1)} async-done(((bf16[64,4608]{1,0:T(8,128)(2,1)}), bf16[512,4608]{1,0:T(8,128)(2,1)}) %all-gather.10.cloned.1.call-update) | async-done | bytes 4718608 | tf_op jit(solution)/shard_map/all_gather | solution.py:508
  130.5 2.5 fusion.2
  133.0 42.6 %all-gather.16.cloned.1.call-done = bf16[1,2048,512]{2,1,0:T(8,128)(2,1)} async-done(((bf16[1,512,512]{2,1,0:T(8,128)(2,1)}), bf16[1,2048,512]{2,1,0:T(8,128)(2,1)}) %all-gather.16.cloned.1.call-update) | async-done | bytes 2097168 | tf_op jit(solution)/shard_map/all_gather | solution.py:510
  175.6 22.7 %shard_map.238 = (f32[512,512]{1,0:T(8,128)}, bf16[512,512]{1,0:T(8,128)(2,1)}, bf16[2048,512]{1,0:T(8,128)(2,1)}, bf16[2048,512]{1,0:T(8,128)(2,1)}, bf16[512,512]{1,0:T(8,128)(2,1)}, /*index=5*/f32[512,128]{1,0:T(8,128)}) custom-call(s32[1]{0:T(128)} %bitcast.d_ref, s32[1]{0:T(128)S(6)} %copy.76.lim_ref, bf16[512,512]{1,0:T(8,128)(2,1)} %get-tuple-element.39.att_ref, ...), custom_call_target="tpu_custom_call" | custom-call | flops 12000000000 | bytes 10485760 | tf_op jit(solution)/shard_map/pallas_call | solution.py:466
  198.4 3.2 slice.124.wup_ref
  201.6 2.5 all-gather.12.cloned.1.call-done.wdn_ref
  204.0 14.7 %shard_map.239 = (bf16[256,512]{1,0:T(8,128)(2,1)}, bf16[256,512]{1,0:T(8,128)(2,1)}, f32[512,512]{1,0:T(8,128)}, bf16[512,512]{1,0:T(8,128)(2,1)}, bf16[8,4,64,...) custom-call(f32[512,512]{1,0:T(8,128)} %get-tuple-element.40.res1_ref, ...), custom_call_target="tpu_custom_call" | custom-call | flops 8000000000 | bytes 10485760 | tf_op jit(solution)/shard_map/pallas_call | solution.py:466
  218.7 37.4 %shard_map.240 = (bf16[2048,512]{1,0:T(8,128)(2,1)}, f32[512,512]{1,0:T(8,128)}, bf16[512,512]{1,0:T(8,128)(2,1)}, bf16[8,4,64,512]{3,2,1,0:T(8,128)(2,1)}, f32[16,512]{1,0:T(8,128)}) custom-call(s32[1]{0:T(128)S(6)} %copy.76.lim_ref, bf16[512,512]{1,0:T(8,128)(2,1)} %get-tuple-element.47.cq_ref, bf16[2048,512]{1,0:T(8,128)(2,1)} %get-tuple-element.48.ek_ref, ...), custom_call_target="tpu_custom_call" | custom-call | flops 24000000000 | bytes 10485760 | tf_op jit(solution)/shard_map/pallas_call | solution.py:466
  256.2 27.9 %shard_map.241 = (bf16[2048,512]{1,0:T(8,128)(2,1)}, bf16[8,4,64,384]{3,2,1,0:T(8,128)(2,1)}, f32[16,512]{1,0:T(8,128)}) custom-call(s32[1]{0:T(128)} %bitcast.d_ref, bf16[512,512]{1,0:T(8,128)(2,1)} %get-tuple-element.44.q_ref, bf16[2048,512]{1,0:T(8,128)(2,1)} %get-tuple-element.45.k_ref, bf16[2048,512]{1,0:T(8,128)(2,1)} %get-tuple-element.46.v_ref, ...), custom_call_target="tpu_custom_call" | custom-call | flops 16000000000 | bytes 10485760 | tf_op jit(solution)/shard_map/pallas_call | solution.py:466
  285.7 43.3 %reduce-scatter.13.cloned.1.call-done = bf16[1,4,64,384]{3,2,1,0:T(8,128)(2,1)} async-done(((bf16[8,4,64,384]{3,2,1,0:T(8,128)(2,1)}), bf16[1,4,64,384]{3,2,1,0:T(8,128)(2,1)}) %reduce-scatter.13.cloned.1.call-update) | async-done | bytes 196624 | tf_op jit(solution)/shard_map/reduce_scatter | solution.py:578
  329.1 44.4 %reduce-scatter.17.cloned.1.call-done = bf16[1,4,64,512]{3,2,1,0:T(8,128)(2,1)} async-done(((bf16[8,4,64,512]{3,2,1,0:T(8,128)(2,1)}), bf16[1,4,64,512]{3,2,1,0:T(8,128)(2,1)}) %reduce-scatter.17.cloned.1.call-update) | async-done | bytes 262160 | tf_op jit(solution)/shard_map/reduce_scatter | solution.py:578
  378.2 7.0 %collective-permute-start.3 = (bf16[256,512]{1,0:T(8,128)(2,1)S(1)}, bf16[256,512]{1,0:T(8,128)(2,1)S(1)}, u32[]{:S(2)}, u32[]{:S(2)}) collective-permute-start(bf16[256,512]{1,0:T(8,128)(2,1)S(1)} %copy-done.5), channel_id=1, source_target_pairs={{1,0},{3,1},{2,2},{0,3},{5,4},{7,5},{6,6},{4,7},{9,8},{11,9},{10,1... | collective-permute-start | bytes 786440 | tf_op jit(solution)/shard_map/ppermute | solution.py:572
  385.2 22.9 %all-reduce = bf16[8,4,272]{2,1,0:T(4,128)(2,1)S(1)} all-reduce(bf16[8,4,272]{2,1,0:T(4,128)(2,1)S(1)} %copy.69), channel_id=12, replica_groups=mesh['dp'=8,'sp'=4] {'dp'}, use_global_device_ids=true, to_apply=%region_8.0.clone | all-reduce | flops 8704 | bytes 34816
  408.7 10.9 %all-reduce.1 = bf16[4,272]{1,0:T(4,128)(2,1)S(1)} all-reduce(bf16[4,272]{1,0:T(4,128)(2,1)S(1)} %dynamic-slice_bitcast_fusion), channel_id=13, replica_groups=mesh['dp'=8,'sp'=4] {'sp'}, use_global_device_ids=true, to_apply=%region_9.0.clone | all-reduce | flops 1088 | bytes 4352
  423.8 7.5 %reduce-scatter.21.cloned.1.call-done = bf16[1,4,64,1152]{3,2,1,0:T(8,128)(2,1)} async-done(((bf16[8,4,64,1152]{3,2,1,0:T(8,128)(2,1)}), bf16[1,4,64,1152]{3,2,1,0:T(8,128)(2,1)}) %reduce-scatter.21.cloned.1.call-update) | async-done | bytes 589840 | tf_op jit(solution)/shard_map/reduce_scatter | solution.py:578
  431.3 21.6 %reduce-scatter.15.cloned.1.call-done = bf16[1,64,384]{2,1,0:T(8,128)(2,1)} async-done(((bf16[4,64,384]{2,1,0:T(8,128)(2,1)}), bf16[1,64,384]{2,1,0:T(8,128)(2,1)}) %reduce-scatter.15.cloned.1.call-update) | async-done | bytes 49168 | tf_op jit(solution)/shard_map/reduce_scatter | solution.py:579
  454.4 18.7 %reduce-scatter.19.cloned.1.call-done = bf16[1,64,512]{2,1,0:T(8,128)(2,1)} async-done(((bf16[4,64,512]{2,1,0:T(8,128)(2,1)}), bf16[1,64,512]{2,1,0:T(8,128)(2,1)}) %reduce-scatter.19.cloned.1.call-update) | async-done | bytes 65552 | tf_op jit(solution)/shard_map/reduce_scatter | solution.py:579
  475.2 42.3 %reduce-scatter.9.cloned.1.call-done = bf16[512,512]{1,0:T(8,128)(2,1)} async-done(((bf16[2048,512]{1,0:T(8,128)(2,1)}), bf16[512,512]{1,0:T(8,128)(2,1)}) %reduce-scatter.9.cloned.1.call-update) | async-done | bytes 524304 | tf_op jit(solution)/shard_map/reduce_scatter | solution.py:575
  519.7 43.3 %reduce-scatter.11.cloned.1.call-done = bf16[512,512]{1,0:T(8,128)(2,1)} async-done(((bf16[2048,512]{1,0:T(8,128)(2,1)}), bf16[512,512]{1,0:T(8,128)(2,1)}) %reduce-scatter.11.cloned.1.call-update) | async-done | bytes 524304 | tf_op jit(solution)/shard_map/reduce_scatter | solution.py:574
  565.1 21.5 %reduce-scatter.23.cloned.1.call-done = bf16[1,64,1152]{2,1,0:T(8,128)(2,1)} async-done(((bf16[4,64,1152]{2,1,0:T(8,128)(2,1)}), bf16[1,64,1152]{2,1,0:T(8,128)(2,1)}) %reduce-scatter.23.cloned.1.call-update) | async-done | bytes 147472 | tf_op jit(solution)/shard_map/reduce_scatter | solution.py:579
  (103 shorter events, 39.4 us)
Async XLA Ops:
  7.2 8.5 %copy-start.3 = (bf16[64,2048]{1,0:T(8,128)(2,1)S(1)}, bf16[64,2048]{1,0:T(8,128)(2,1)}, u32[]{:S(2)}) copy-start(bf16[64,2048]{1,0:T(8,128)(2,1)} %param.22) | copy-start | bytes 786436
  7.2 10.6 %copy-start.2 = (bf16[1,512,512]{2,1,0:T(8,128)(2,1)S(1)}, bf16[1,512,512]{2,1,0:T(8,128)(2,1)}, u32[]{:S(2)}) copy-start(bf16[1,512,512]{2,1,0:T(8,128)(2,1)} %param.16) | copy-start | bytes 1572868
  7.2 33.4 %all-gather.8.cloned.1.call-start = ((), (), s32[]{:S(2)}) async-start(), calls=%async_computation.8 | async-start | bytes 1916928 | tf_op jit(solution)/shard_map/all_gather | solution.py:505
  11.5 76.6 %all-gather.14.cloned.1.call-start = ((), (), s32[]{:S(2)}) async-start(), calls=%async_computation.19 | async-start | bytes 2621440 | tf_op jit(solution)/shard_map/all_gather | solution.py:506
  12.2 116.0 %all-gather.10.cloned.1.call-start = ((), (), s32[]{:S(2)}) async-start(), calls=%async_computation.9 | async-start | bytes 5308416 | tf_op jit(solution)/shard_map/all_gather | solution.py:508
  16.6 159.0 %all-gather.16.cloned.1.call-start = ((), (), s32[]{:S(2)}) async-start(), calls=%async_computation.20 | async-start | bytes 2621440 | tf_op jit(solution)/shard_map/all_gather | solution.py:510
  17.2 186.9 %all-gather.12.cloned.1.call-start = ((), (), s32[]{:S(2)}) async-start(), calls=%async_computation.10 | async-start | bytes 2359296 | tf_op jit(solution)/shard_map/all_gather | solution.py:509
  17.8 311.2 %reduce-scatter.13.cloned.1.call-start = ((), (), s32[]{:S(2)}) async-start(), calls=%async_computation.13 | async-start | bytes 1769472 | tf_op jit(solution)/shard_map/reduce_scatter | solution.py:578
  17.9 183.7 %collective-permute-start = (bf16[256,512]{1,0:T(8,128)(2,1)S(1)}, bf16[256,512]{1,0:T(8,128)(2,1)S(1)}, u32[]{:S(2)}, u32[]{:S(2)}) collective-permute-start(bf16[256,512]{1,0:T(8,128)(2,1)S(1)} %get-tuple-element.69), channel_id=1, source_target_pairs={{0,0},{1,2},{2,3},{3,1},{4,4},{5,6},{6,7},{7,5},{8,8},{9,10},{10,1... | collective-permute-start | bytes 786440 | tf_op jit(solution)/shard_map/ppermute | solution.py:512
  18.5 183.0 %collective-permute-start.1 = (bf16[256,512]{1,0:T(8,128)(2,1)S(1)}, bf16[256,512]{1,0:T(8,128)(2,1)S(1)}, u32[]{:S(2)}, u32[]{:S(2)}) collective-permute-start(bf16[256,512]{1,0:T(8,128)(2,1)S(1)} %get-tuple-element.68), channel_id=1, source_target_pairs={{0,1},{1,3},{2,2},{3,0},{4,5},{5,7},{6,6},{7,4},{8,9},{9,11},{10,1... | collective-permute-start | bytes 786440 | tf_op jit(solution)/shard_map/ppermute | solution.py:513
  40.6 2.9 copy-start
  201.5 2.5 copy-start.7
  201.5 2.5 copy-start.8
  284.2 89.3 %reduce-scatter.17.cloned.1.call-start = ((), (), s32[]{:S(2)}) async-start(), calls=%async_computation.15 | async-start | bytes 2359296 | tf_op jit(solution)/shard_map/reduce_scatter | solution.py:578
  284.9 146.4 %reduce-scatter.21.cloned.1.call-start = ((), (), s32[]{:S(2)}) async-start(), calls=%async_computation.17 | async-start | bytes 5308416 | tf_op jit(solution)/shard_map/reduce_scatter | solution.py:578
  285.7 167.3 %reduce-scatter.15.cloned.1.call-start = ((), (), s32[]{:S(2)}) async-start(), calls=%async_computation.14 | async-start | bytes 245760 | tf_op jit(solution)/shard_map/reduce_scatter | solution.py:579
  329.0 144.1 %reduce-scatter.19.cloned.1.call-start = ((), (), s32[]{:S(2)}) async-start(), calls=%async_computation.16 | async-start | bytes 327680 | tf_op jit(solution)/shard_map/reduce_scatter | solution.py:579
  373.5 144.0 %reduce-scatter.9.cloned.1.call-start = ((), (), s32[]{:S(2)}) async-start(), calls=%async_computation.11 | async-start | bytes 2621440 | tf_op jit(solution)/shard_map/reduce_scatter | solution.py:575
  373.6 3.9 copy-start.6
  373.6 4.6 copy-start.5
  374.2 188.7 %reduce-scatter.11.cloned.1.call-start = ((), (), s32[]{:S(2)}) async-start(), calls=%async_computation.12 | async-start | bytes 2621440 | tf_op jit(solution)/shard_map/reduce_scatter | solution.py:574
  374.8 211.8 %reduce-scatter.23.cloned.1.call-start = ((), (), s32[]{:S(2)}) async-start(), calls=%async_computation.18 | async-start | bytes 737280 | tf_op jit(solution)/shard_map/reduce_scatter | solution.py:579
  377.5 45.5 %collective-permute-start.2 = (bf16[256,512]{1,0:T(8,128)(2,1)S(1)}, bf16[256,512]{1,0:T(8,128)(2,1)S(1)}, u32[]{:S(2)}, u32[]{:S(2)}) collective-permute-start(bf16[256,512]{1,0:T(8,128)(2,1)S(1)} %copy-done.6), channel_id=1, source_target_pairs={{0,0},{2,1},{3,2},{1,3},{4,4},{6,5},{7,6},{5,7},{8,8},{10,9},{11,1... | collective-permute-start | bytes 786440 | tf_op jit(solution)/shard_map/ppermute | solution.py:572
  378.2 44.8 %collective-permute-start.3 = (bf16[256,512]{1,0:T(8,128)(2,1)S(1)}, bf16[256,512]{1,0:T(8,128)(2,1)S(1)}, u32[]{:S(2)}, u32[]{:S(2)}) collective-permute-start(bf16[256,512]{1,0:T(8,128)(2,1)S(1)} %copy-done.5), channel_id=1, source_target_pairs={{1,0},{3,1},{2,2},{0,3},{5,4},{7,5},{6,6},{4,7},{9,8},{11,9},{10,1... | collective-permute-start | bytes 786440 | tf_op jit(solution)/shard_map/ppermute | solution.py:572
  (4 other events, 6.5 us)
Sparse Core Ops, SparseCore 0:
  11.6 28.9 all-gather.7
  42.1 45.9 all-gather.13
  90.6 37.6 all-gather.9
  129.7 45.9 all-gather.15
  177.4 26.6 all-gather.11
  284.3 44.6 reduce-scatter.12
  332.3 41.1 reduce-scatter.16
  377.3 53.9 reduce-scatter.20
  433.6 19.3 reduce-scatter.14
  455.2 17.8 reduce-scatter.18
  475.4 42.1 reduce-scatter.8
  519.8 43.1 reduce-scatter.10
  565.3 21.3 reduce-scatter.22
